TPU v7x, 1024 devices: a whole 4x4x32 slice. The times are simulated.
1024 devices in a mesh: dp: 16 (over z_lo, core), mp: 64 (over y, x, z_hi).
Axes of the slice: x: 4, y: 4, z: 32 (z_hi: 4, z_lo: 8; z = z_hi * 8 + z_lo), core: 2. Of those that a mesh axis runs over, the one named last changes fastest.
Arguments:
- hidden_rows: bfloat16 [3008, 8192], P('dp'), may hold values from -6 to 6
- query_weight: bfloat16 [8192, 8192], P('dp', 'mp'), may hold values from -0.0625 to 0.0625
- output_weight: bfloat16 [8192, 8192], P('mp'), may hold values from -0.375 to 0.375
- new_kv: bfloat16 [2, 3008, 1024], P(None, 'dp'), may hold values from -6 to 6
- prefix_kv: bfloat16 [2, 752, 8, 16, 128], P(None, 'dp'), may hold values from -300 to 300
- adapter_bank: bfloat16 [752, 2, 8, 8192], P('dp', None, None, 'mp'), may hold values from -0.69921875 to 0.69921875
- send_plan: int32 [16, 16, 5], P('dp'), may hold values from 0 to 46, as said below
- user_slot: int32 [752], P('dp'), may hold values from 0 to 79, as said below
Outputs:
- mixed: bfloat16 [3008, 8192], P('dp', 'mp')
Inputs may be any that keep to these rules, and one draw needn't show every extreme that they name: send_plan[s, g, c] is an index into owner group s's 47 adapters. Slots c below the number of g's users served by s name distinct adapters; the other slots hold valid indices that no user reads. Each of an owner's adapters is read by exactly one user. user_slot[u] = s * 5 + c means the adapter of user u (of row group g = u // 47) is send_plan[s, g, c] of owner group s. Users of one group have distinct slots and use their owner's slots from c = 0 upward. The number of group g's users served by owner s depends only on (s - g) mod 16; it is exactly 5 at distance 0 and at one or more other distances, and at most 5 everywhere.
All inputs are finite; a program needn't handle non-finite values.
Results may differ from a plain program's by a relative error of at most 0.009.
Values may be sent and summed in bfloat16 or wider, within the bound.
A program may use at most 64 MiB of HBM per device.

v0:
```python
import math

import jax
import jax.numpy as jnp
from jax import lax
from jax.sharding import PartitionSpec as P

SAMPLES = 4
GROUP = 8


def body(
    hidden_rows, query_weight, output_weight, new_kv, prefix_kv, adapter_bank, send_plan, user_slot
):
    row_count = hidden_rows.shape[0]
    user_count = row_count // SAMPLES
    head_dim = prefix_kv.shape[4]
    heads_here = output_weight.shape[0] // head_dim
    width_here = heads_here * head_dim
    kv_count = max(1, heads_here // GROUP)
    per_kv = heads_here // kv_count
    score_scale = 1.0 / math.sqrt(head_dim)
    queries = jnp.dot(
        hidden_rows,
        lax.all_gather(query_weight, "dp", axis=0, tiled=True),
        preferred_element_type=jnp.float32,
    ).astype(jnp.bfloat16)
    outgoing = adapter_bank[send_plan[0]]
    incoming = lax.all_to_all(outgoing, "dp", split_axis=0, concat_axis=0, tiled=True)
    received = incoming.reshape((incoming.shape[0] * incoming.shape[1],) + incoming.shape[2:])
    user_blocks = received[user_slot]
    kv_first = lax.axis_index("mp") * heads_here // GROUP
    cache_here = lax.dynamic_slice_in_dim(prefix_kv, kv_first, kv_count, 2)
    fresh_here = lax.dynamic_slice_in_dim(new_kv, kv_first * head_dim, kv_count * head_dim, 2)
    query_heads = queries.reshape(user_count, SAMPLES, kv_count, per_kv, head_dim)
    own_keys = fresh_here[0].reshape(user_count, SAMPLES, kv_count, head_dim)
    own_values = fresh_here[1].reshape(user_count, SAMPLES, kv_count, head_dim)
    cached = (
        jnp.einsum(
            "uskgd,ukpd->uskgp", query_heads, cache_here[0], preferred_element_type=jnp.float32
        )
        * score_scale
    )
    own_score = (
        jnp.einsum("uskgd,uskd->uskg", query_heads, own_keys, preferred_element_type=jnp.float32)
        * score_scale
    )
    row_top = jnp.maximum(jnp.max(cached, axis=-1), own_score)
    cached_exp = jnp.exp(cached - row_top[..., None])
    own_exp = jnp.exp(own_score - row_top)
    weight_total = jnp.sum(cached_exp, axis=-1) + own_exp
    cached_weight = (cached_exp / weight_total[..., None]).astype(jnp.bfloat16)
    own_weight = (own_exp / weight_total).astype(jnp.bfloat16)
    mixed_values = jnp.einsum(
        "uskgp,ukpd->uskgd", cached_weight, cache_here[1], preferred_element_type=jnp.float32
    )
    mixed_values = (
        mixed_values
        + own_weight.astype(jnp.float32)[..., None]
        * own_values.astype(jnp.float32)[:, :, :, None, :]
    )
    attended = mixed_values.astype(jnp.bfloat16).reshape(row_count, width_here)
    grouped = attended.reshape(user_count, SAMPLES, width_here)
    rank_part = jnp.einsum(
        "usk,urk->usr", grouped, user_blocks[:, 0], preferred_element_type=jnp.float32
    )
    rank_vector = lax.psum(rank_part, "mp").astype(jnp.bfloat16)
    adapter_out = jnp.einsum(
        "usr,urk->usk", rank_vector, user_blocks[:, 1], preferred_element_type=jnp.float32
    )
    adapter_out = adapter_out.reshape(row_count, adapter_out.shape[2])
    partial_out = jnp.dot(attended, output_weight, preferred_element_type=jnp.float32)
    base_out = lax.psum_scatter(partial_out, "mp", scatter_dimension=1, tiled=True)
    return (base_out + adapter_out).astype(jnp.bfloat16)


def solution(mesh):
    return jax.shard_map(
        body,
        mesh=mesh,
        in_specs=(
            P("dp", None),
            P("dp", "mp"),
            P("mp", None),
            P(None, "dp", None),
            P(None, "dp", None, None, None),
            P("dp", None, None, "mp"),
            P("dp", None, None),
            P("dp"),
        ),
        out_specs=P("dp", "mp"),
        check_vma=False,
    )
```

profile of v0, /device:TPU:32, one launch (start us, length us, event | category | flops | bytes accessed | tf_op | source)
XLA Modules:
  0.0 790.0 jit_solution(287335232214727546)
XLA Ops:
  6.5 0.0 copy-start
  6.5 0.0 all-gather.2.cloned.1.call-start
  6.5 0.7 all-gather.2.cloned.1.call-update
  7.3 0.0 reduce-scatter.2.cloned.1.call-start
  7.3 1.5 dynamic-slice_reduce_fusion
  8.9 112.8 %all-gather.2.cloned.1.call-done = bf16[8192,128]{1,0:T(8,128)(2,1)} async-done(((bf16[512,128]{1,0:T(8,128)(2,1)}), bf16[8192,128]{1,0:T(8,128)(2,1)}) %all-gather.2.cloned.1.call-update) | async-done | bytes 2097168 | tf_op jit(solution)/shard_map/all_gather | solution.py:25
  121.6 0.0 copy-done
  121.6 2.6 convolution_convert_fusion
  124.2 0.1 fusion.5
  124.4 1.2 fusion.15
  125.6 0.2 fusion.6
  125.9 1.2 fusion.2
  127.1 5.2 fusion.16
  132.4 0.0 copy-start.2
  132.4 0.0 copy-start.1
  132.4 0.0 copy-start.3
  132.4 0.0 reduce-scatter.2.cloned.1.call-update
  132.4 0.7 copy-done.2
  133.1 0.1 copy.12
  133.1 0.1 reshape.122
  133.2 0.1 copy-done.1
  133.3 1.4 gather_fusion
  134.7 16.6 %all-to-all-start = ((bf16[16,5,2,8,128]{4,3,2,1,0:T(8,128)(2,1)}), bf16[16,5,2,8,128]{4,3,2,1,0:T(8,128)(2,1)S(1)}, u32[]{:S(2)}, u32[]{:S(2)}) async-start(bf16[16,5,2,8,128]{4,3,2,1,0:T(8,128)(2,1)} %bitcast.11), calls=%async_computation.1 | async-start | bytes 655360 | tf_op jit(solution)/shard_map/all_to_all | solution.py:29
  151.3 0.0 copy-done.3
  151.3 18.0 %all-to-all-done = bf16[16,5,2,8,128]{4,3,2,1,0:T(8,128)(2,1)S(1)} async-done(((bf16[16,5,2,8,128]{4,3,2,1,0:T(8,128)(2,1)}), bf16[16,5,2,8,128]{4,3,2,1,0:T(8,128)(2,1)S(1)}, u32[]{:S(2)}, u32[]{:S(2)}) %all-to-all-start) | async-done | bytes 327712 | tf_op jit(solution)/shard_map/all_to_all | solution.py:29
  169.3 1.3 gather_fusion.1
  170.5 1.1 fusion.4
  171.6 608.9 %psum.7 = bf16[47,4,8]{2,1,0:T(4,128)(2,1)S(1)} all-reduce(f32[47,4,8]{2,1,0:T(4,128)S(1)} %fusion.4), channel_id=1, replica_groups=mesh['dp'=16,'mp'=64] {'mp'}, use_global_device_ids=true, to_apply=%region_3.4 | all-reduce | flops 1504 | bytes 9024 | tf_op jit(solution)/shard_map/psum | solution.py:67
  780.5 1.1 fusion.3
  781.6 0.0 reduce-scatter.2.cloned.1.call-done
  781.7 1.5 add_convert_fusion
  (10 shorter events, 0.2 us)
Async XLA Ops:
  6.5 115.1 %copy-start = (bf16[188,8192]{1,0:T(8,128)(2,1)S(1)}, bf16[188,8192]{1,0:T(8,128)(2,1)}, u32[]{:S(2)}) copy-start(bf16[188,8192]{1,0:T(8,128)(2,1)} %param.8) | copy-start | bytes 9240580
  6.5 115.1 %all-gather.2.cloned.1.call-start = ((), (), s32[]{:S(2)}) async-start(), calls=%async_computation.2 | async-start | bytes 2228224 | tf_op jit(solution)/shard_map/all_gather | solution.py:25
  7.3 774.4 %reduce-scatter.2.cloned.1.call-start = ((), (), s32[]{:S(2)}) async-start(), calls=%async_computation.3 | async-start | bytes 6389760 | tf_op jit(solution)/shard_map/reduce_scatter | solution.py:73
  132.4 0.7 copy-start.2
  132.4 0.9 copy-start.1
  132.4 18.9 %copy-start.3 = (s32[47]{0:T(128)S(1)}, s32[47]{0:T(128)}, u32[]{:S(2)}) copy-start(s32[47]{0:T(128)} %param.15) | copy-start | bytes 568
  134.7 34.6 %all-to-all-start = ((bf16[16,5,2,8,128]{4,3,2,1,0:T(8,128)(2,1)}), bf16[16,5,2,8,128]{4,3,2,1,0:T(8,128)(2,1)S(1)}, u32[]{:S(2)}, u32[]{:S(2)}) async-start(bf16[16,5,2,8,128]{4,3,2,1,0:T(8,128)(2,1)} %bitcast.11), calls=%async_computation.1 | async-start | bytes 655360 | tf_op jit(solution)/shard_map/all_to_all | solution.py:29
Sparse Core Ops, SparseCore 0:
  10.0 111.5 all-gather.1
  132.5 578.7 reduce-scatter.1
where the time goes:
time: 790 us
  blocking collectives  609 us (77%)
  waiting for transfers between devices  131 us (17%)
  starting transfers between devices  16.6 us (2%)
  between operations  13.6 us (2%)
  matrix products  12.4 us (2%)
    psum x1, blocking collectives, body(): rank_vector = lax.psum(rank_part, 'mp').astype(jnp.bfloat16)  609 us
    all_gather x1, waiting for transfers between devices, body(): lax.all_gather(query_weight, 'dp', axis=0, tiled=True)  113 us
    all_to_all x1, waiting for transfers between devices, body(): lax.all_to_all(outgoing, 'dp', split_axis=0, concat_axis=0, tiled=True)  18 us
    all_to_all x1, starting transfers between devices, body(): lax.all_to_all(outgoing, 'dp', split_axis=0, concat_axis=0, tiled=True)  16.6 us
  transfers between devices with their start and end apart: 3, of which 2 were waited for; matrix products, arithmetic and copies ran while one was open for 1% of the time, Pallas kernels for 0%

commit v1 on v0

v1 whole, which is shorter than its diff:
```python
import functools
import math

import jax
import jax.numpy as jnp
from jax import lax
from jax.experimental import pallas as pl
from jax.experimental.pallas import tpu as pltpu
from jax.sharding import PartitionSpec as P

SAMPLES = 4
GROUP = 8
CAP = 5
CORES = 2
Z_HI = 4
CHUNKS = 2
F32 = jnp.float32
BF16 = jnp.bfloat16


def each(first, last, step):
    def wrapped(i, carry):
        step(i)
        return carry

    lax.fori_loop(first, last, wrapped, 0)


def kernel(
    group,
    plan_ref, slot_ref, hid_hbm, qw_hbm, ow_hbm, new_hbm, prefix_hbm, bank_hbm,
    out_ref,
    hid, qbuf, acc, wbuf, fresh, cache, bank, give, take, qrows, att, part, zsend, zrecv,
    rank_xy, rank_z,
    local_sem, up_send, up_recv, down_send, down_recv, sib_send, sib_recv,
    w_send, w_recv, wsib_send, wsib_recv, give_send, take_recv, att_send, att_recv,
    z_send, z_recv, rxy_send, rxy_recv, rz_send, rz_recv,
):
    n_dp = qbuf.shape[0]
    n_xy = wbuf.shape[0]
    n_line = n_dp // CORES
    rows = hid.shape[0]
    shard = qbuf.shape[1]
    hd = qbuf.shape[2]
    users = cache.shape[1]
    prefix = cache.shape[2]
    pad_rows = att.shape[1]
    half = hd // CORES
    wide = wbuf.shape[2]
    bit = shard // CHUNKS

    me = lax.axis_index("dp")
    mp = lax.axis_index("mp")
    z, core = me // CORES, me % CORES
    spot, z_hi = mp // Z_HI, mp % Z_HI
    twin = z * CORES + (1 - core)
    kv = mp // group

    def dp_peer(d):
        return (me + d) % n_dp

    def xy_peer(d):
        return ((spot + d) % n_xy) * Z_HI + z_hi

    def z_peer(d):
        return spot * Z_HI + (z_hi + d) % Z_HI

    loads = [
        pltpu.make_async_copy(hid_hbm, hid, local_sem.at[0]),
        pltpu.make_async_copy(qw_hbm, qbuf.at[me], local_sem.at[1]),
        pltpu.make_async_copy(
            ow_hbm.at[:, pl.ds(pl.multiple_of(spot * wide, wide), wide)], wbuf.at[spot], local_sem.at[2]
        ),
        pltpu.make_async_copy(
            new_hbm.at[:, :, pl.ds(pl.multiple_of(kv * hd, hd), hd)], fresh, local_sem.at[3]
        ),
        pltpu.make_async_copy(prefix_hbm.at[:, :, kv], cache.at[:, pl.ds(0, prefix_hbm.shape[1])], local_sem.at[4]),
        pltpu.make_async_copy(bank_hbm, bank, local_sem.at[5]),
    ]
    for load in loads:
        load.start()

    barrier = pltpu.get_barrier_semaphore()

    def greet(peer):
        pl.semaphore_signal(barrier, inc=1, device_id=peer, device_id_type=pl.DeviceIdType.MESH)

    each(1, n_dp, lambda d: greet({"dp": dp_peer(d)}))
    each(1, n_xy, lambda d: greet({"mp": xy_peer(d)}))
    each(1, Z_HI, lambda d: greet({"mp": z_peer(d)}))
    pl.semaphore_wait(barrier, n_dp + n_xy + Z_HI - 3)

    def remote(src, dst, send_sem, recv_sem, peer):
        return pltpu.make_async_remote_copy(
            src_ref=src, dst_ref=dst, send_sem=send_sem, recv_sem=recv_sem,
            device_id=peer, device_id_type=pl.DeviceIdType.MESH,
        )

    def piece(origin, b):
        return qbuf.at[origin * CORES + core, pl.ds(b * bit, bit)]

    def up(i, b, src=None):
        dst = piece(z - i, b)
        return remote(dst if src is None else src, dst, up_send.at[i, b], up_recv.at[i, b], {"dp": me + CORES})

    def down(i, b, src=None):
        dst = piece(z + i, b)
        return remote(dst if src is None else src, dst, down_send.at[i, b], down_recv.at[i, b], {"dp": me - CORES})

    def across(origin, b, src=None):
        dst = piece(origin, b)
        return remote(dst if src is None else src, dst, sib_send.at[origin, b], sib_recv.at[origin, b], {"dp": twin})

    def out_weight(d):
        peer = (spot + d) % n_xy
        return remote(
            ow_hbm.at[pl.ds(core * half, half), pl.ds(pl.multiple_of(peer * wide, wide), wide)],
            wbuf.at[spot, pl.ds(core * half, half)],
            w_send.at[d], w_recv.at[d], {"mp": peer * Z_HI + z_hi},
        )

    def out_weight_across(d):
        origin = (spot + n_xy - d) % n_xy
        where = wbuf.at[origin, pl.ds(core * half, half)]
        return remote(where, where, wsib_send.at[d], wsib_recv.at[d], {"dp": twin})

    for b in range(CHUNKS):
        src = qw_hbm.at[pl.ds(b * bit, bit)]

        @pl.when(z < n_line - 1)
        def _():
            up(0, b, src).start()

        @pl.when(z > 0)
        def _():
            down(0, b, src).start()

    for b in range(CHUNKS):
        across(z, b, qw_hbm.at[pl.ds(b * bit, bit)]).start()

    loads[5].wait()

    def pick(i):
        give[i // CAP, pl.ds(pl.multiple_of(i % CAP * 16, 16), 16), :] = bank[plan_ref[i // CAP, i % CAP]]

    each(0, n_dp * CAP, pick)
    take[me] = give[me]

    loads[0].wait()
    loads[1].wait()
    acc[...] = jnp.zeros_like(acc)

    def multiply(origin):
        columns = pl.ds(pl.multiple_of(origin * shard, shard), shard)
        acc[...] += jnp.dot(hid[:, columns], qbuf[origin], preferred_element_type=F32)

    def multiply_twin(origin):
        for b in range(CHUNKS):
            across(origin, b).wait_recv()
        multiply(origin * CORES + 1 - core)

    multiply(me)
    w_each = -(-(n_xy - 1) // (n_line - 1))

    def line_step(i):
        for b in range(CHUNKS):

            @pl.when(z - i >= 0)
            def _():
                up(i - 1, b).wait_recv()

                @pl.when(z < n_line - 1)
                def _():
                    up(i, b).start()

                across(z - i, b).start()

            @pl.when(z + i < n_line)
            def _():
                down(i - 1, b).wait_recv()

                @pl.when(z > 0)
                def _():
                    down(i, b).start()

                across(z + i, b).start()

        for k in range(w_each):
            d = (i - 1) * w_each + 1 + k

            @pl.when(d < n_xy)
            def _():
                out_weight(d).start()

        @pl.when(z - i >= 0)
        def _():
            multiply((z - i) * CORES + core)

        @pl.when(z + i < n_line)
        def _():
            multiply((z + i) * CORES + core)

        @pl.when(z - i + 1 >= 0)
        def _():
            multiply_twin(z - i + 1)

        @pl.when((z + i - 1 < n_line) & (i > 1))
        def _():
            multiply_twin(z + i - 1)

    each(1, n_line, line_step)

    @pl.when(z == n_line - 1)
    def _():
        multiply_twin(0)

    @pl.when(z == 0)
    def _():
        multiply_twin(n_line - 1)

    def adapters(d):
        peer = dp_peer(d)
        return remote(give.at[peer], take.at[me], give_send.at[d], take_recv.at[d], {"dp": peer})

    each(1, n_dp, lambda d: adapters(d).start())

    def pass_weight(d):
        out_weight(d).wait_recv()
        out_weight_across(d).start()

    each(1, n_xy, pass_weight)

    loads[3].wait()
    loads[4].wait()
    if pad_rows > rows:
        cache[:, prefix_hbm.shape[1] :] = jnp.zeros_like(cache[:, prefix_hbm.shape[1] :])
        qrows[...] = jnp.zeros_like(qrows)
    qrows[0, 0:rows, :] = acc[...].astype(BF16).astype(F32)
    qrows[1, 0:rows, :] = fresh[:, 0, :].astype(F32)
    qrows[2, 0:rows, :] = fresh[:, 1, :].astype(F32)
    block = 8
    tall, keys = block * SAMPLES, block * prefix
    score_scale = 1.0 / math.sqrt(hd)
    own_user = lax.broadcasted_iota(jnp.int32, (tall, keys), 0) // SAMPLES == (
        lax.broadcasted_iota(jnp.int32, (tall, keys), 1) // prefix
    )
    for n in range(users // block):
        at = slice(n * tall, (n + 1) * tall)
        query = qrows[0, at, :]
        key = cache[0, n * block : (n + 1) * block].reshape(keys, hd)
        value = cache[1, n * block : (n + 1) * block].reshape(keys, hd)
        cached = (
            lax.dot_general(query.astype(BF16), key, (((1,), (1,)), ((), ())), preferred_element_type=F32)
            * score_scale
        )
        own_score = jnp.sum(query * qrows[1, at, :], axis=-1, keepdims=True) * score_scale
        cached = jnp.where(own_user, cached, -jnp.inf)
        row_top = jnp.maximum(jnp.max(cached, axis=-1, keepdims=True), own_score)
        cached_exp = jnp.exp(cached - row_top)
        own_exp = jnp.exp(own_score - row_top)
        weight_total = jnp.sum(cached_exp, axis=-1, keepdims=True) + own_exp
        cached_weight = (cached_exp / weight_total).astype(BF16)
        own_weight = (own_exp / weight_total).astype(BF16).astype(F32)
        mixed = jnp.dot(cached_weight, value, preferred_element_type=F32) + own_weight * qrows[2, at, :]
        att[spot, at, :] = mixed.astype(BF16)

    def attended(d):
        return remote(att.at[spot], att.at[spot], att_send.at[d], att_recv.at[d], {"mp": xy_peer(d)})

    each(1, n_xy, lambda d: attended(d).start())
    loads[2].wait()
    each(1, n_xy, lambda d: out_weight_across(d).wait_recv())
    each(1, n_xy, lambda d: attended(d).wait_recv())
    for n in range(0, n_xy, 2):
        left = jnp.concatenate([att[n], att[n + 1]], axis=1)
        right = jnp.concatenate([wbuf[n], wbuf[n + 1]], axis=0)
        term = jnp.dot(left, right, preferred_element_type=F32)
        if n == 0:
            part[...] = term
        else:
            part[...] += term
    for n in range(Z_HI):
        zsend[n] = part[:, n * hd : (n + 1) * hd].astype(BF16)

    def partial_sum(d):
        return remote(zsend.at[(z_hi + d) % Z_HI], zrecv.at[d], z_send.at[d], z_recv.at[d], {"mp": z_peer(d)})

    each(1, Z_HI, lambda d: partial_sum(d).start())

    lane_user = lax.broadcasted_iota(jnp.int32, (1, pad_rows), 1) // SAMPLES

    def place(u, row):
        return jnp.where(lane_user == u, slot_ref[u], row)

    row_slot = lax.fori_loop(0, rows // SAMPLES, place, jnp.full((1, pad_rows), -1, jnp.int32))
    each(1, n_dp, lambda d: adapters(d).wait_recv())
    slots = n_dp * CAP
    maps = take[...].reshape(slots * 16, hd)
    products = lax.dot_general(maps, att[spot], (((1,), (1,)), ((), ())), preferred_element_type=F32)
    products = products.reshape(slots, 16, pad_rows)[:, 0:8, :]
    slot_of = lax.broadcasted_iota(jnp.int32, (slots, 8, pad_rows), 0)
    rank_xy[spot] = jnp.sum(jnp.where(slot_of == row_slot[None], products, 0.0), axis=0)

    def rank_over_xy(d):
        return remote(rank_xy.at[spot], rank_xy.at[spot], rxy_send.at[d], rxy_recv.at[d], {"mp": xy_peer(d)})

    def rank_over_z(d):
        return remote(rank_z.at[z_hi], rank_z.at[z_hi], rz_send.at[d], rz_recv.at[d], {"mp": z_peer(d)})

    each(1, n_xy, lambda d: rank_over_xy(d).start())
    each(1, n_xy, lambda d: rank_over_xy(d).wait_recv())
    rank_z[z_hi] = jnp.sum(rank_xy[...], axis=0)
    each(1, Z_HI, lambda d: rank_over_z(d).start())
    each(1, Z_HI, lambda d: rank_over_z(d).wait_recv())
    rank = jnp.sum(rank_z[...], axis=0).astype(BF16).astype(F32)
    rank = jnp.concatenate([jnp.zeros_like(rank), rank], axis=0)
    slot_of = lax.broadcasted_iota(jnp.int32, (slots, 16, pad_rows), 0)
    spread = jnp.where(slot_of == row_slot[None], rank[None], 0.0).astype(BF16).reshape(slots * 16, pad_rows)
    total = lax.dot_general(spread, maps, (((0,), (0,)), ((), ())), preferred_element_type=F32)
    total += part[:, pl.ds(pl.multiple_of(z_hi * hd, hd), hd)]
    each(1, Z_HI, lambda d: partial_sum(d).wait_recv())
    for d in range(1, Z_HI):
        total += zrecv[d].astype(F32)
    out_ref[...] = total[0:rows].astype(BF16)

    for b in range(CHUNKS):
        for i in range(n_line):

            @pl.when((z < n_line - 1) & (z - i >= 0))
            def _():
                up(i, b).wait_send()

            @pl.when((z > 0) & (z + i < n_line))
            def _():
                down(i, b).wait_send()

        each(0, n_line, lambda o: across(o, b).wait_send())

    def sent(d):
        out_weight(d).wait_send()
        out_weight_across(d).wait_send()
        attended(d).wait_send()
        rank_over_xy(d).wait_send()

    each(1, n_xy, sent)
    each(1, n_dp, lambda d: adapters(d).wait_send())
    each(1, Z_HI, lambda d: partial_sum(d).wait_send())
    each(1, Z_HI, lambda d: rank_over_z(d).wait_send())


def body(
    n_dp, n_mp,
    hidden_rows, query_weight, output_weight, new_kv, prefix_kv, adapter_bank, send_plan, user_slot,
):
    rows = hidden_rows.shape[0]
    shard, hd = query_weight.shape
    n_xy, n_line = n_mp // Z_HI, n_dp // CORES
    prefix = prefix_kv.shape[3]
    users = -(-(rows // SAMPLES) // 8) * 8
    pad_rows = users * SAMPLES
    wide = output_weight.shape[1] // n_xy
    owned = adapter_bank.shape[0]
    bank = adapter_bank.reshape(owned, 16, hd)
    dma = pltpu.SemaphoreType.DMA
    hbm = pl.BlockSpec(memory_space=pl.ANY)
    smem = pl.BlockSpec(memory_space=pltpu.SMEM)
    vmem = pl.BlockSpec(memory_space=pltpu.VMEM)
    return pl.pallas_call(
        functools.partial(kernel, GROUP),
        out_shape=jax.ShapeDtypeStruct((rows, hd), BF16),
        in_specs=[smem, smem, hbm, hbm, hbm, hbm, hbm, hbm],
        out_specs=vmem,
        scratch_shapes=[
            pltpu.VMEM(hidden_rows.shape, BF16),
            pltpu.VMEM((n_dp, shard, hd), BF16),
            pltpu.VMEM((rows, hd), F32),
            pltpu.VMEM((n_xy, hd, wide), BF16),
            pltpu.VMEM((rows, 2, hd), BF16),
            pltpu.VMEM((2, users, prefix, hd), BF16),
            pltpu.VMEM((owned, 16, hd), BF16),
            pltpu.VMEM((n_dp, CAP * 16, hd), BF16),
            pltpu.VMEM((n_dp, CAP * 16, hd), BF16),
            pltpu.VMEM((3, pad_rows, hd), F32),
            pltpu.VMEM((n_xy, pad_rows, hd), BF16),
            pltpu.VMEM((pad_rows, wide), F32),
            pltpu.VMEM((Z_HI, pad_rows, hd), BF16),
            pltpu.VMEM((Z_HI, pad_rows, hd), BF16),
            pltpu.VMEM((n_xy, 8, pad_rows), F32),
            pltpu.VMEM((Z_HI, 8, pad_rows), F32),
            dma((6,)),
            dma((n_line, CHUNKS)),
            dma((n_line, CHUNKS)),
            dma((n_line, CHUNKS)),
            dma((n_line, CHUNKS)),
            dma((n_line, CHUNKS)),
            dma((n_line, CHUNKS)),
            dma((n_xy,)),
            dma((n_xy,)),
            dma((n_xy,)),
            dma((n_xy,)),
            dma((n_dp,)),
            dma((n_dp,)),
            dma((n_xy,)),
            dma((n_xy,)),
            dma((Z_HI,)),
            dma((Z_HI,)),
            dma((n_xy,)),
            dma((n_xy,)),
            dma((Z_HI,)),
            dma((Z_HI,)),
        ],
        compiler_params=pltpu.CompilerParams(
            collective_id=0, has_side_effects=True, vmem_limit_bytes=60 * 1024 * 1024
        ),
    )(send_plan[0], user_slot, hidden_rows, query_weight, output_weight, jnp.transpose(new_kv, (1, 0, 2)), prefix_kv, bank)


def solution(mesh):
    return jax.shard_map(
        functools.partial(body, mesh.shape["dp"], mesh.shape["mp"]),
        mesh=mesh,
        in_specs=(
            P("dp", None),
            P("dp", "mp"),
            P("mp", None),
            P(None, "dp", None),
            P(None, "dp", None, None, None),
            P("dp", None, None, "mp"),
            P("dp", None, None),
            P("dp"),
        ),
        out_specs=P("dp", "mp"),
        check_vma=False,
    )
```

time: 790 us -> 104 us (0.13)
  the two profiles are of different devices: /device:TPU:32 before, /device:TPU:17 now
where the time goes in v1:
time: 104 us
  Pallas kernels  101 us (97%)
  local copies, waits for them, and re-layouts  2.78 us (3%)
    pallas_call x1, Pallas kernels, body(): pl.pallas_call(functools.partial(kernel, GROUP), out_shape=jax.ShapeDtype...  101 us

profile of v1, /device:TPU:17, one launch (start us, length us, event | category | flops | bytes accessed | tf_op | source)
XLA Modules:
  0.0 104.2 jit_solution(10509800830336451596)
XLA Ops:
  0.0 1.4 %copy.10 = s32[1,16,5]{2,1,0:T(8,128)} copy(s32[1,16,5]{1,0,2:T(1,128)} %param.14) | data formatting | bytes 640 | tf_op jit(solution)/shard_map/squeeze | solution.py:415
  1.4 101.4 %shard_map.82 = bf16[188,128]{1,0:T(8,128)(2,1)} custom-call(s32[16,5]{1,0:T(8,128)} %bitcast.5, s32[47]{0:T(128)} %slot_ref.1, bf16[188,8192]{1,0:T(8,128)(2,1)} %hid_hbm.1, bf16[512,128]{1,0:T(8,128)(2,1)} %qw_hbm.1, bf16[128,8192]{1,0:T(8,128)(2,1)} %ow_hbm.1, bf16[188,2,1024]{2,1,0:T(2,128)(2,1)} %bitcast.3, bf16[2,47,8,16,128]{4,3,2,1,0:T(8,128)(2,1)} %prefix_hbm.1, ...), custom_call_target="tpu_custom_call" | custom-call | tf_op jit(solution)/shard_map/pallas_call | solution.py:368
  102.8 1.4 %copy.12 = bf16[188,128]{1,0:T(8,128)(2,1)} copy(bf16[188,128]{1,0:T(8,128)(2,1)} %shard_map.82) | data formatting | bytes 96256

commit v2 on v1

--- a/solution.py
+++ b/solution.py
@@ -13,7 +13,8 @@
 CAP = 5
 CORES = 2
 Z_HI = 4
-CHUNKS = 2
+CHUNKS = 4
+HALVES = 2
 F32 = jnp.float32
 BF16 = jnp.bfloat16
 
@@ -34,7 +35,7 @@
     rank_xy, rank_z,
     local_sem, up_send, up_recv, down_send, down_recv, sib_send, sib_recv,
     w_send, w_recv, wsib_send, wsib_recv, give_send, take_recv, att_send, att_recv,
-    z_send, z_recv, rxy_send, rxy_recv, rz_send, rz_recv,
+    z_send, z_recv, rxy_send, rxy_recv, rz_send, rz_recv, ring_sem,
 ):
     n_dp = qbuf.shape[0]
     n_xy = wbuf.shape[0]
@@ -85,10 +86,32 @@
     def greet(peer):
         pl.semaphore_signal(barrier, inc=1, device_id=peer, device_id_type=pl.DeviceIdType.MESH)
 
-    each(1, n_dp, lambda d: greet({"dp": dp_peer(d)}))
+    n_ring = n_line * Z_HI
+
+    def ring_peer(d):
+        at = (z_hi * n_line + z + d + n_ring) % n_ring
+        return {"dp": at % n_line * CORES + core, "mp": spot * Z_HI + at // n_line}
+
+    greet(ring_peer(1))
+    greet(ring_peer(-1))
+    greet({"dp": twin})
     each(1, n_xy, lambda d: greet({"mp": xy_peer(d)}))
-    each(1, Z_HI, lambda d: greet({"mp": z_peer(d)}))
-    pl.semaphore_wait(barrier, n_dp + n_xy + Z_HI - 3)
+    pl.semaphore_wait(barrier, n_xy + 2)
+
+    stages = ring_sem.shape[0]
+
+    def tell(k):
+        for d in (2**k, -(2**k)):
+            pl.semaphore_signal(
+                ring_sem.at[k], inc=1, device_id=ring_peer(d), device_id_type=pl.DeviceIdType.MESH
+            )
+
+    def heard(k):
+        pl.semaphore_wait(ring_sem.at[k], 2)
+        if k + 1 < stages:
+            tell(k + 1)
+
+    tell(0)
 
     def remote(src, dst, send_sem, recv_sem, peer):
         return pltpu.make_async_remote_copy(
@@ -141,7 +164,7 @@
     loads[5].wait()
 
     def pick(i):
-        give[i // CAP, pl.ds(pl.multiple_of(i % CAP * 16, 16), 16), :] = bank[plan_ref[i // CAP, i % CAP]]
+        give[i // CAP, pl.ds(pl.multiple_of(i % CAP * 16, 16), 16), :] = bank[plan_ref[i % CAP, 0, i // CAP]]
 
     each(0, n_dp * CAP, pick)
     take[me] = give[me]
@@ -151,15 +174,12 @@
     acc[...] = jnp.zeros_like(acc)
 
     def multiply(origin):
-        columns = pl.ds(pl.multiple_of(origin * shard, shard), shard)
-        acc[...] += jnp.dot(hid[:, columns], qbuf[origin], preferred_element_type=F32)
-
-    def multiply_twin(origin):
         for b in range(CHUNKS):
             across(origin, b).wait_recv()
-        multiply(origin * CORES + 1 - core)
-
-    multiply(me)
+        columns = pl.ds(pl.multiple_of(origin * CORES * shard, CORES * shard), CORES * shard)
+        pair = qbuf[pl.ds(origin * CORES, CORES)].reshape(CORES * shard, hd)
+        acc[...] += jnp.dot(hid[:, columns], pair, preferred_element_type=F32)
+
     w_each = -(-(n_xy - 1) // (n_line - 1))
 
     def line_step(i):
@@ -185,6 +205,25 @@
 
                 across(z + i, b).start()
 
+            if b == CHUNKS // 2 - 1:
+
+                @pl.when(z - i + 1 >= 0)
+                def _():
+                    multiply(z - i + 1)
+
+            if b == CHUNKS - 1:
+
+                @pl.when((z + i - 1 < n_line) & (i > 1))
+                def _():
+                    multiply(z + i - 1)
+
+        for k in range(stages):
+            if 2**k < n_line:
+
+                @pl.when(i == 2**k)
+                def _():
+                    heard(k)
+
         for k in range(w_each):
             d = (i - 1) * w_each + 1 + k
 
@@ -192,31 +231,19 @@
             def _():
                 out_weight(d).start()
 
-        @pl.when(z - i >= 0)
-        def _():
-            multiply((z - i) * CORES + core)
-
-        @pl.when(z + i < n_line)
-        def _():
-            multiply((z + i) * CORES + core)
-
-        @pl.when(z - i + 1 >= 0)
-        def _():
-            multiply_twin(z - i + 1)
-
-        @pl.when((z + i - 1 < n_line) & (i > 1))
-        def _():
-            multiply_twin(z + i - 1)
-
     each(1, n_line, line_step)
 
     @pl.when(z == n_line - 1)
     def _():
-        multiply_twin(0)
+        multiply(0)
 
     @pl.when(z == 0)
     def _():
-        multiply_twin(n_line - 1)
+        multiply(n_line - 1)
+
+    for k in range(stages):
+        if 2**k >= n_line:
+            heard(k)
 
     def adapters(d):
         peer = dp_peer(d)
@@ -264,35 +291,48 @@
         mixed = jnp.dot(cached_weight, value, preferred_element_type=F32) + own_weight * qrows[2, at, :]
         att[spot, at, :] = mixed.astype(BF16)
 
-    def attended(d):
-        return remote(att.at[spot], att.at[spot], att_send.at[d], att_recv.at[d], {"mp": xy_peer(d)})
-
-    each(1, n_xy, lambda d: attended(d).start())
+    half_rows = pad_rows // HALVES
+
+    def attended(h, d):
+        at = att.at[spot, pl.ds(h * half_rows, half_rows)]
+        return remote(at, at, att_send.at[h, d], att_recv.at[h, d], {"mp": xy_peer(d)})
+
+    def partial_sum(h, d):
+        target = (z_hi + d) % Z_HI
+        return remote(zsend.at[h, target], zrecv.at[h, d], z_send.at[h, d], z_recv.at[h, d], {"mp": z_peer(d)})
+
+    def project(h):
+        each(1, n_xy, lambda d: attended(h, d).wait_recv())
+        at = slice(h * half_rows, (h + 1) * half_rows)
+        for n in range(0, n_xy, 2):
+            left = jnp.concatenate([att[n, at], att[n + 1, at]], axis=1)
+            right = jnp.concatenate([wbuf[n], wbuf[n + 1]], axis=0)
+            term = jnp.dot(left, right, preferred_element_type=F32)
+            if n == 0:
+                part[at] = term
+            else:
+                part[at] += term
+        for n in range(Z_HI):
+            zsend[h, n] = part[at, n * hd : (n + 1) * hd].astype(BF16)
+
+    def send_sums(h):
+        for d in (2, 1, 3):
+            partial_sum(h, d).start()
+
+    for h in range(HALVES):
+        each(1, n_xy, lambda d: attended(h, d).start())
     loads[2].wait()
-    each(1, n_xy, lambda d: out_weight_across(d).wait_recv())
-    each(1, n_xy, lambda d: attended(d).wait_recv())
-    for n in range(0, n_xy, 2):
-        left = jnp.concatenate([att[n], att[n + 1]], axis=1)
-        right = jnp.concatenate([wbuf[n], wbuf[n + 1]], axis=0)
-        term = jnp.dot(left, right, preferred_element_type=F32)
-        if n == 0:
-            part[...] = term
-        else:
-            part[...] += term
-    for n in range(Z_HI):
-        zsend[n] = part[:, n * hd : (n + 1) * hd].astype(BF16)
-
-    def partial_sum(d):
-        return remote(zsend.at[(z_hi + d) % Z_HI], zrecv.at[d], z_send.at[d], z_recv.at[d], {"mp": z_peer(d)})
-
-    each(1, Z_HI, lambda d: partial_sum(d).start())
-
     lane_user = lax.broadcasted_iota(jnp.int32, (1, pad_rows), 1) // SAMPLES
 
     def place(u, row):
         return jnp.where(lane_user == u, slot_ref[u], row)
 
     row_slot = lax.fori_loop(0, rows // SAMPLES, place, jnp.full((1, pad_rows), -1, jnp.int32))
+    each(1, n_xy, lambda d: out_weight_across(d).wait_recv())
+    for h in range(HALVES - 1):
+        project(h)
+        send_sums(h)
+
     each(1, n_dp, lambda d: adapters(d).wait_recv())
     slots = n_dp * CAP
     maps = take[...].reshape(slots * 16, hd)
@@ -308,9 +348,12 @@
         return remote(rank_z.at[z_hi], rank_z.at[z_hi], rz_send.at[d], rz_recv.at[d], {"mp": z_peer(d)})
 
     each(1, n_xy, lambda d: rank_over_xy(d).start())
+    project(HALVES - 1)
     each(1, n_xy, lambda d: rank_over_xy(d).wait_recv())
     rank_z[z_hi] = jnp.sum(rank_xy[...], axis=0)
-    each(1, Z_HI, lambda d: rank_over_z(d).start())
+    for d in (2, 1, 3):
+        rank_over_z(d).start()
+    send_sums(HALVES - 1)
     each(1, Z_HI, lambda d: rank_over_z(d).wait_recv())
     rank = jnp.sum(rank_z[...], axis=0).astype(BF16).astype(F32)
     rank = jnp.concatenate([jnp.zeros_like(rank), rank], axis=0)
@@ -318,10 +361,13 @@
     spread = jnp.where(slot_of == row_slot[None], rank[None], 0.0).astype(BF16).reshape(slots * 16, pad_rows)
     total = lax.dot_general(spread, maps, (((0,), (0,)), ((), ())), preferred_element_type=F32)
     total += part[:, pl.ds(pl.multiple_of(z_hi * hd, hd), hd)]
-    each(1, Z_HI, lambda d: partial_sum(d).wait_recv())
-    for d in range(1, Z_HI):
-        total += zrecv[d].astype(F32)
-    out_ref[...] = total[0:rows].astype(BF16)
+    for h in range(HALVES):
+        at = slice(h * half_rows, min((h + 1) * half_rows, rows))
+        some = total[at]
+        for d in (1, 3, 2):
+            partial_sum(h, d).wait_recv()
+            some += zrecv[h, d, 0 : at.stop - at.start].astype(F32)
+        out_ref[at] = some.astype(BF16)
 
     for b in range(CHUNKS):
         for i in range(n_line):
@@ -339,12 +385,13 @@
     def sent(d):
         out_weight(d).wait_send()
         out_weight_across(d).wait_send()
-        attended(d).wait_send()
         rank_over_xy(d).wait_send()
 
     each(1, n_xy, sent)
     each(1, n_dp, lambda d: adapters(d).wait_send())
-    each(1, Z_HI, lambda d: partial_sum(d).wait_send())
+    for h in range(HALVES):
+        each(1, n_xy, lambda d: attended(h, d).wait_send())
+        each(1, Z_HI, lambda d: partial_sum(h, d).wait_send())
     each(1, Z_HI, lambda d: rank_over_z(d).wait_send())
 
 
@@ -383,8 +430,8 @@
             pltpu.VMEM((3, pad_rows, hd), F32),
             pltpu.VMEM((n_xy, pad_rows, hd), BF16),
             pltpu.VMEM((pad_rows, wide), F32),
-            pltpu.VMEM((Z_HI, pad_rows, hd), BF16),
-            pltpu.VMEM((Z_HI, pad_rows, hd), BF16),
+            pltpu.VMEM((HALVES, Z_HI, pad_rows // HALVES, hd), BF16),
+            pltpu.VMEM((HALVES, Z_HI, pad_rows // HALVES, hd), BF16),
             pltpu.VMEM((n_xy, 8, pad_rows), F32),
             pltpu.VMEM((Z_HI, 8, pad_rows), F32),
             dma((6,)),
@@ -400,19 +447,20 @@
             dma((n_xy,)),
             dma((n_dp,)),
             dma((n_dp,)),
+            dma((HALVES, n_xy)),
+            dma((HALVES, n_xy)),
+            dma((HALVES, Z_HI)),
+            dma((HALVES, Z_HI)),
             dma((n_xy,)),
             dma((n_xy,)),
             dma((Z_HI,)),
             dma((Z_HI,)),
-            dma((n_xy,)),
-            dma((n_xy,)),
-            dma((Z_HI,)),
-            dma((Z_HI,)),
+            pltpu.SemaphoreType.REGULAR(((2 * n_line).bit_length() - 1,)),
         ],
         compiler_params=pltpu.CompilerParams(
             collective_id=0, has_side_effects=True, vmem_limit_bytes=60 * 1024 * 1024
         ),
-    )(send_plan[0], user_slot, hidden_rows, query_weight, output_weight, jnp.transpose(new_kv, (1, 0, 2)), prefix_kv, bank)
+    )(jnp.transpose(send_plan, (2, 0, 1)), user_slot, hidden_rows, query_weight, output_weight, jnp.transpose(new_kv, (1, 0, 2)), prefix_kv, bank)
 
 
 def solution(mesh):

time: 104 us -> 91.3 us (0.88)
  the two profiles are of different devices: /device:TPU:17 before, /device:TPU:193 now
where the time goes in v2:
time: 91.3 us; the launch traced here: 91.1 us
  Pallas kernels  89.7 us (98%)
  local copies, waits for them, and re-layouts  1.42 us (2%)
    pallas_call x1, Pallas kernels, body(): pl.pallas_call(functools.partial(kernel, GROUP), out_shape=jax.ShapeDtype...  89.7 us

profile of v2, /device:TPU:193, one launch (start us, length us, event | category | flops | bytes accessed | tf_op | source)
XLA Modules:
  0.0 91.1 jit_solution(13900805369250819693)
XLA Ops:
  0.0 89.7 %shard_map.82 = bf16[188,128]{1,0:T(8,128)(2,1)} custom-call(s32[5,1,16]{2,1,0:T(1,128)} %bitcast.5, s32[47]{0:T(128)} %slot_ref.1, bf16[188,8192]{1,0:T(8,128)(2,1)} %hid_hbm.1, bf16[512,128]{1,0:T(8,128)(2,1)} %qw_hbm.1, bf16[128,8192]{1,0:T(8,128)(2,1)} %ow_hbm.1, bf16[188,2,1024]{2,1,0:T(2,128)(2,1)} %bitcast.3, bf16[2,47,8,16,128]{4,3,2,1,0:T(8,128)(2,1)} %prefix_hbm.1, ...), custom_call_target="tpu_custom_call" | custom-call | tf_op jit(solution)/shard_map/pallas_call | solution.py:415
  89.7 1.4 %copy.10 = bf16[188,128]{1,0:T(8,128)(2,1)} copy(bf16[188,128]{1,0:T(8,128)(2,1)} %shard_map.82) | data formatting | bytes 96256

commit v3 on v2

--- a/solution.py
+++ b/solution.py
@@ -15,6 +15,7 @@
 Z_HI = 4
 CHUNKS = 4
 HALVES = 2
+LANES = 128
 F32 = jnp.float32
 BF16 = jnp.bfloat16
 
@@ -35,7 +36,7 @@
     rank_xy, rank_z,
     local_sem, up_send, up_recv, down_send, down_recv, sib_send, sib_recv,
     w_send, w_recv, wsib_send, wsib_recv, give_send, take_recv, att_send, att_recv,
-    z_send, z_recv, rxy_send, rxy_recv, rz_send, rz_recv, ring_sem,
+    z_send, z_recv, rxy_send, rxy_recv, rz_send, rz_recv, ring_sem, maps_f32, user_up,
 ):
     n_dp = qbuf.shape[0]
     n_xy = wbuf.shape[0]
@@ -161,6 +162,8 @@
     for b in range(CHUNKS):
         across(z, b, qw_hbm.at[pl.ds(b * bit, bit)]).start()
 
+    each(1, n_xy, lambda d: out_weight(d).start())
+
     loads[5].wait()
 
     def pick(i):
@@ -180,8 +183,6 @@
         pair = qbuf[pl.ds(origin * CORES, CORES)].reshape(CORES * shard, hd)
         acc[...] += jnp.dot(hid[:, columns], pair, preferred_element_type=F32)
 
-    w_each = -(-(n_xy - 1) // (n_line - 1))
-
     def line_step(i):
         for b in range(CHUNKS):
 
@@ -223,13 +224,6 @@
                 @pl.when(i == 2**k)
                 def _():
                     heard(k)
-
-        for k in range(w_each):
-            d = (i - 1) * w_each + 1 + k
-
-            @pl.when(d < n_xy)
-            def _():
-                out_weight(d).start()
 
     each(1, n_line, line_step)
 
@@ -302,11 +296,14 @@
         return remote(zsend.at[h, target], zrecv.at[h, d], z_send.at[h, d], z_recv.at[h, d], {"mp": z_peer(d)})
 
     def project(h):
-        each(1, n_xy, lambda d: attended(h, d).wait_recv())
         at = slice(h * half_rows, (h + 1) * half_rows)
         for n in range(0, n_xy, 2):
-            left = jnp.concatenate([att[n, at], att[n + 1, at]], axis=1)
-            right = jnp.concatenate([wbuf[n], wbuf[n + 1]], axis=0)
+            for d in (n, n + 1):
+                if d > 0:
+                    attended(h, d).wait_recv()
+            one, two = (spot + n_xy - n) % n_xy, (spot + n_xy - n - 1) % n_xy
+            left = jnp.concatenate([att[one, at], att[two, at]], axis=1)
+            right = jnp.concatenate([wbuf[one], wbuf[two]], axis=0)
             term = jnp.dot(left, right, preferred_element_type=F32)
             if n == 0:
                 part[at] = term
@@ -354,12 +351,54 @@
     for d in (2, 1, 3):
         rank_over_z(d).start()
     send_sums(HALVES - 1)
+
+    maps_f32[0 : slots * 16, :] = maps.astype(F32)
+    maps_f32[slots * 16 :, :] = jnp.zeros_like(maps_f32[slots * 16 :, :])
+    row_user = lax.broadcasted_iota(jnp.int32, (pad_rows, LANES), 0) // SAMPLES
+
+    def place_rows(u, rows_slot):
+        return jnp.where(row_user == u, slot_ref[u], rows_slot)
+
+    rows_slot = lax.fori_loop(0, rows // SAMPLES, place_rows, jnp.full((pad_rows, LANES), -1, jnp.int32))
+    lane = lax.broadcasted_iota(jnp.int32, (pad_rows, LANES), 1)
+    pick_slot = jnp.where(lane == rows_slot, 1.0, 0.0).astype(BF16)
+    for j in range(8):
+        up_map = maps_f32[pl.ds(8 + j, LANES, stride=16), :].astype(BF16)
+        user_up[j] = jnp.dot(pick_slot, up_map, preferred_element_type=F32)
+
+    for b in range(CHUNKS):
+        for i in range(n_line):
+
+            @pl.when((z < n_line - 1) & (z - i >= 0))
+            def _():
+                up(i, b).wait_send()
+
+            @pl.when((z > 0) & (z + i < n_line))
+            def _():
+                down(i, b).wait_send()
+
+        each(0, n_line, lambda o: across(o, b).wait_send())
+
+    def sent(d):
+        out_weight(d).wait_send()
+        out_weight_across(d).wait_send()
+        rank_over_xy(d).wait_send()
+
+    each(1, n_xy, sent)
+    each(1, n_dp, lambda d: adapters(d).wait_send())
+    for h in range(HALVES):
+        each(1, n_xy, lambda d: attended(h, d).wait_send())
+
     each(1, Z_HI, lambda d: rank_over_z(d).wait_recv())
-    rank = jnp.sum(rank_z[...], axis=0).astype(BF16).astype(F32)
-    rank = jnp.concatenate([jnp.zeros_like(rank), rank], axis=0)
-    slot_of = lax.broadcasted_iota(jnp.int32, (slots, 16, pad_rows), 0)
-    spread = jnp.where(slot_of == row_slot[None], rank[None], 0.0).astype(BF16).reshape(slots * 16, pad_rows)
-    total = lax.dot_general(spread, maps, (((0,), (0,)), ((), ())), preferred_element_type=F32)
+    rank = jnp.sum(rank_z[...], axis=0)
+    rank = jnp.concatenate([rank, jnp.zeros_like(rank)], axis=0).astype(BF16)
+    which = lax.broadcasted_iota(jnp.int32, (16, 8 * hd), 0)
+    over = lax.broadcasted_iota(jnp.int32, (16, 8 * hd), 1) // hd
+    ones = jnp.where(which == over, 1.0, 0.0).astype(BF16)
+    spread = lax.dot_general(rank, ones, (((0,), (0,)), ((), ())), preferred_element_type=F32)
+    total = spread[:, 0:hd] * user_up[0]
+    for j in range(1, 8):
+        total += spread[:, j * hd : (j + 1) * hd] * user_up[j]
     total += part[:, pl.ds(pl.multiple_of(z_hi * hd, hd), hd)]
     for h in range(HALVES):
         at = slice(h * half_rows, min((h + 1) * half_rows, rows))
@@ -369,31 +408,9 @@
             some += zrecv[h, d, 0 : at.stop - at.start].astype(F32)
         out_ref[at] = some.astype(BF16)
 
-    for b in range(CHUNKS):
-        for i in range(n_line):
-
-            @pl.when((z < n_line - 1) & (z - i >= 0))
-            def _():
-                up(i, b).wait_send()
-
-            @pl.when((z > 0) & (z + i < n_line))
-            def _():
-                down(i, b).wait_send()
-
-        each(0, n_line, lambda o: across(o, b).wait_send())
-
-    def sent(d):
-        out_weight(d).wait_send()
-        out_weight_across(d).wait_send()
-        rank_over_xy(d).wait_send()
-
-    each(1, n_xy, sent)
-    each(1, n_dp, lambda d: adapters(d).wait_send())
     for h in range(HALVES):
-        each(1, n_xy, lambda d: attended(h, d).wait_send())
         each(1, Z_HI, lambda d: partial_sum(h, d).wait_send())
     each(1, Z_HI, lambda d: rank_over_z(d).wait_send())
-
 
 def body(
     n_dp, n_mp,
@@ -456,6 +473,8 @@
             dma((Z_HI,)),
             dma((Z_HI,)),
             pltpu.SemaphoreType.REGULAR(((2 * n_line).bit_length() - 1,)),
+            pltpu.VMEM((LANES * 16 + 16, hd), F32),
+            pltpu.VMEM((8, pad_rows, hd), F32),
         ],
         compiler_params=pltpu.CompilerParams(
             collective_id=0, has_side_effects=True, vmem_limit_bytes=60 * 1024 * 1024

time: 91.3 us -> 90.4 us (level)
  the two profiles are of different devices: /device:TPU:193 before, /device:TPU:226 now
where the time goes in v3:
time: 90.4 us; the launch traced here: 90.2 us
  Pallas kernels  88.8 us (98%)
  local copies, waits for them, and re-layouts  1.42 us (2%)
    pallas_call x1, Pallas kernels, body(): pl.pallas_call(functools.partial(kernel, GROUP), out_shape=jax.ShapeDtype...  88.8 us

profile of v3, /device:TPU:226, one launch (start us, length us, event | category | flops | bytes accessed | tf_op | source)
XLA Modules:
  0.0 90.2 jit_solution(1946208778480716730)
XLA Ops:
  0.0 88.8 %shard_map.82 = bf16[188,128]{1,0:T(8,128)(2,1)} custom-call(s32[5,1,16]{2,1,0:T(1,128)} %bitcast.5, s32[47]{0:T(128)} %slot_ref.1, bf16[188,8192]{1,0:T(8,128)(2,1)} %hid_hbm.1, bf16[512,128]{1,0:T(8,128)(2,1)} %qw_hbm.1, bf16[128,8192]{1,0:T(8,128)(2,1)} %ow_hbm.1, bf16[188,2,1024]{2,1,0:T(2,128)(2,1)} %bitcast.3, bf16[2,47,8,16,128]{4,3,2,1,0:T(8,128)(2,1)} %prefix_hbm.1, ...), custom_call_target="tpu_custom_call" | custom-call | tf_op jit(solution)/shard_map/pallas_call | solution.py:432
  88.8 1.4 %copy.10 = bf16[188,128]{1,0:T(8,128)(2,1)} copy(bf16[188,128]{1,0:T(8,128)(2,1)} %shard_map.82) | data formatting | bytes 96256
